TPU v7x, 32 devices: a whole 2x2x4 slice. The times are simulated.
32 devices in a mesh: groups: 2 (over x), sensor: 16 (over z, y, core).
Axes of the slice: x: 2, y: 2, z: 4, core: 2. Of those that a mesh axis runs over, the one named last changes fastest.
Arguments:
- series: bfloat16 [32, 32, 16384], P(None, None, ('groups', 'sensor')), parts along dimension 2, may hold values from -6 to 6
- caches: bfloat16 [2, 32, 2, 16384], P(None, None, None, ('groups', 'sensor')), parts along dimension 3, may hold values from -6 to 6
- dilation: int32 [2], replicated, may hold values from 1 to 2
- conv_weight: bfloat16 [2, 4, 32, 32], replicated, may hold values from -0.75 to 0.75
- conv_bias: float32 [2, 2, 32], replicated, may hold values from -3 to 3
- mix_weight: bfloat16 [2, 3, 32, 32], replicated, may hold values from -0.75 to 0.75
- mix_bias: float32 [2, 32], replicated, may hold values from -3 to 3
- skip_weight: bfloat16 [2, 256, 32], replicated, may hold values from -1 to 1
- block_cols: int32 [128, 5], P(('groups', 'sensor')), parts along dimension 0, may hold values from 0 to 63, as said below
- block_count: int32 [128], P(('groups', 'sensor')), parts along dimension 0, may hold values from 1 to 5, as said below
- edge_tiles: bfloat16 [128, 5, 128, 128], P(('groups', 'sensor')), parts along dimension 0, may hold values from -0.25 to 0.25
Outputs:
- next_series: bfloat16 [32, 32, 16384], P(None, None, ('groups', 'sensor')), parts along dimension 2
- skip_sum: bfloat16 [256, 8, 16384], P(None, None, ('groups', 'sensor')), parts along dimension 2
There are 2 independent parts, one for each index of `groups`. A program takes and returns all parts, laid end to end along the dimension named above; an argument that names none is the same for every part. Nothing has to cross between parts.
Inputs may be any that keep to these rules, and one draw needn't show every extreme that they name: `block_cols`: slot s of row block r names block (r + o) mod 64 for some o with -2 <= o <= 2; the 5 slots of one row block name distinct blocks. Row block r uses its first block_count[r] slots; the other slots are ignored.
All inputs are finite; a program needn't handle non-finite values.
Results may differ from a plain program's by a relative error of at most 0.0057.
Values may be sent and summed in bfloat16 or wider, within the bound.
A program may use at most 64 MiB of HBM per device.

v0:
```python
import functools

import jax
import jax.numpy as jnp
from jax import lax
from jax.experimental import pallas as pl
from jax.experimental.pallas import tpu as pltpu
from jax.sharding import PartitionSpec as P

LAYERS = 2
DMAX = 2
SKT = 8
LANES = 128
CHUNK = 8
GROUP = 4
HALF = 16
BF = jnp.bfloat16
F32 = jnp.float32


def dot(a, b):
    return jnp.dot(a, b, preferred_element_type=F32)


def iota(shape, dim):
    return lax.broadcasted_iota(jnp.int32, shape, dim)


def ones_where(mask):
    return jnp.where(mask, 1.0, 0.0).astype(BF)


def spread(weight, rows, columns):
    o, c = weight.shape
    tall = ones_where(iota((rows, o), 0) % o == iota((rows, o), 1))
    wide = ones_where(iota((c, columns), 1) % c == iota((c, columns), 0))
    return dot(tall, dot(weight, wide).astype(BF))


def column(row_vector, rows):
    c = row_vector.shape[1]
    mask = iota((rows, c), 0) % c == iota((rows, c), 1)
    return jnp.sum(jnp.where(mask, row_vector, 0.0), axis=1, keepdims=True)


def kernel(
    total_blocks,
    ring,
    series,
    caches,
    dilation,
    conv_weight,
    conv_bias,
    mix_weight,
    mix_bias,
    skip_weight,
    block_cols,
    block_count,
    edge_tiles,
    next_out,
    skip_out,
    ext,
    xbuf,
    ybuf,
    plan,
    conv_w,
    conv_b,
    mix_w,
    mix_b,
    skip_w,
    send_sem,
    recv_sem,
):
    channels, steps, width = series.shape
    blocks = width // LANES
    reach = (block_cols.shape[1] - 1) // 2
    pairs = blocks // 2
    rows = CHUNK * channels
    chunks = steps // CHUNK
    own = reach
    me = lax.axis_index("sensor")
    left, right = lax.rem(me + ring - 1, ring), lax.rem(me + 1, ring)

    barrier = pltpu.get_barrier_semaphore()
    for other in (left, right):
        pl.semaphore_signal(
            barrier, inc=1, device_id={"sensor": other}, device_id_type=pl.DeviceIdType.MESH
        )

    def halo(e, k):
        at = pl.ds(pl.multiple_of(k * rows, rows), rows)
        out = []
        for side, (target, source, landing) in enumerate(
            ((right, own + blocks - reach, 0), (left, own, own + blocks))
        ):
            out.append(
                pltpu.make_async_remote_copy(
                    src_ref=ext.at[e, pl.ds(source, reach), at, :],
                    dst_ref=ext.at[e, pl.ds(landing, reach), at, :],
                    send_sem=send_sem.at[e, k, side],
                    recv_sem=recv_sem.at[e, k, side],
                    device_id={"sensor": target},
                    device_id_type=pl.DeviceIdType.MESH,
                )
            )
        return out

    def build_conv(l):
        shape = (GROUP * channels, (GROUP + DMAX) * channels)
        to, ti = iota(shape, 0) // channels, iota(shape, 1) // channels
        late = ti == to + DMAX
        early = ti == to + DMAX - dilation[l]
        n = GROUP * channels
        for g in range(2):
            value = jnp.where(early, spread(conv_weight[l, 2 * g], *shape), 0.0) + jnp.where(
                late, spread(conv_weight[l, 2 * g + 1], *shape), 0.0
            )
            conv_w[l, pl.ds(g * n, n), :] = value.astype(BF)
            conv_b[l, pl.ds(g * n, n), :] = column(conv_bias[l, pl.ds(g, 1), :], n)

    def build_mix(l):
        diagonal = iota((rows, rows), 0) // channels == iota((rows, rows), 1) // channels
        for j in range(3):
            value = jnp.where(diagonal, spread(mix_weight[l, j], rows, rows), 0.0)
            mix_w[l, j] = value.astype(BF)
        mix_b[l] = column(mix_bias[pl.ds(l, 1), :], rows)

    def build_skip(l):
        o, c = skip_weight.shape[1:]
        piece = 512
        wide = ones_where(iota((c, SKT * c), 1) % c == iota((c, SKT * c), 0))
        repeated = dot(skip_weight[l], wide).astype(BF)

        def step(i, carry):
            tall = ones_where(
                iota((piece, o), 0) // SKT + i * (piece // SKT) == iota((piece, o), 1)
            )
            mask = iota((piece, SKT * c), 0) % SKT == iota((piece, SKT * c), 1) // c
            at = pl.ds(pl.multiple_of(i * piece, piece), piece)
            skip_w[l, at, :] = jnp.where(mask, dot(tall, repeated), 0.0).astype(BF)
            return carry

        lax.fori_loop(0, o * SKT // piece, step, 0)

    def build_plan():
        plan[...] = jnp.zeros_like(plan)
        nonzero = block_cols.shape[1]
        for r in range(blocks):
            row = me * blocks + r
            where = [
                lax.rem(block_cols[r, s] - row + reach + total_blocks, total_blocks)
                for s in range(nonzero)
            ]
            for o in range(nonzero):
                value = jnp.zeros((LANES, LANES), F32)
                for s in range(nonzero):
                    live = jnp.logical_and(where[s] == o, block_count[r] > s)
                    scale = jnp.where(live, 1.0, 0.0).astype(F32)
                    value = value + scale * edge_tiles[r, s].astype(F32)
                plan[
                    r // 2,
                    pl.ds((r % 2 + o) * LANES, LANES),
                    pl.ds((r % 2) * LANES, LANES),
                ] = value.T.astype(BF)

    def gated(l, e, k):
        n = GROUP * channels
        for g in range(CHUNK // GROUP):
            start = pl.multiple_of(k * rows + g * n, n)
            for q in range(pairs):
                cols = pl.ds(q * 2 * LANES, 2 * LANES)
                x = xbuf[l, pl.ds(start, (GROUP + DMAX) * channels), cols]
                both = dot(conv_w[l], x) + conv_b[l]
                gate = 0.5 * jnp.tanh(0.5 * both[n:]) + 0.5
                hidden = (jnp.tanh(both[:n]) * gate).astype(BF)
                ext[e, own + 2 * q, pl.ds(start, n), :] = hidden[:, :LANES]
                ext[e, own + 2 * q + 1, pl.ds(start, n), :] = hidden[:, LANES:]

    def diffused(e, k, q):
        at = pl.ds(pl.multiple_of(k * rows, rows), rows)
        source = jnp.concatenate(
            [ext[e, 2 * q + j, at, :] for j in range(2 * reach + 2)], axis=1
        )
        return dot(source, plan[q]).astype(BF)

    def first(e, k):
        at = pl.ds(pl.multiple_of(k * rows, rows), rows)
        for q in range(pairs):
            value = diffused(e, k, q)
            ext[e + 1, own + 2 * q, at, :] = value[:, :LANES]
            ext[e + 1, own + 2 * q + 1, at, :] = value[:, LANES:]

    def pair_of(e, k, q):
        at = pl.ds(pl.multiple_of(k * rows, rows), rows)
        return jnp.concatenate(
            [ext[e, own + 2 * q, at, :], ext[e, own + 2 * q + 1, at, :]], axis=1
        )

    def mixed(l, e, k, q):
        cols = pl.ds(q * 2 * LANES, 2 * LANES)
        second = diffused(e + 1, k, q)
        value = (
            dot(mix_w[l, 0], pair_of(e, k, q))
            + dot(mix_w[l, 1], pair_of(e + 1, k, q))
            + dot(mix_w[l, 2], second)
            + mix_b[l]
        )
        at = pl.ds(pl.multiple_of(k * rows + DMAX * channels, channels), rows)
        return (xbuf[l, at, cols].astype(F32) + value).astype(BF)

    def start_halo(e, k):
        for copy in halo(e, k):
            copy.start()

    def wait_halo(e, k):
        for copy in halo(e, k):
            copy.wait_recv()

    def each(body):
        def step(k, carry):
            body(k)
            return carry

        lax.fori_loop(0, chunks, step, 0)

    half_rows = HALF * channels
    square = (half_rows, half_rows)
    for l in range(LAYERS):
        xbuf[l, pl.ds(0, DMAX * channels), :] = caches[l]
    build_conv(0)
    i0, i1 = iota(square, 0), iota(square, 1)
    forward = ones_where((i0 % channels) * HALF + i0 // channels == i1)
    for h in range(steps // HALF):
        piece = series[:, pl.ds(h * HALF, HALF), :].reshape(half_rows, width)
        xbuf[0, pl.ds(DMAX * channels + h * half_rows, half_rows), :] = dot(
            forward, piece
        ).astype(BF)

    pl.semaphore_wait(barrier, 2)

    def hidden_zero(k):
        gated(0, 0, k)
        start_halo(0, k)

    each(hidden_zero)
    build_plan()
    build_conv(1)
    build_mix(0)

    def first_zero(k):
        wait_halo(0, k)
        first(0, k)
        start_halo(1, k)

    each(first_zero)
    build_mix(1)
    build_skip(0)

    def second_zero(k):
        wait_halo(1, k)
        at = pl.ds(pl.multiple_of(k * rows + DMAX * channels, channels), rows)
        for q in range(pairs):
            xbuf[1, at, pl.ds(q * 2 * LANES, 2 * LANES)] = mixed(0, 0, k, q)
        gated(1, 2, k)
        start_halo(2, k)

    each(second_zero)
    build_skip(1)

    def first_one(k):
        wait_halo(2, k)
        first(2, k)
        start_halo(3, k)

    each(first_one)

    piece = 256
    count = skip_out.shape[0] // piece

    def skip_step(i, carry):
        at = pl.ds(pl.multiple_of(i * piece, piece), piece)
        for q in range(pairs):
            value = dot(skip_w[0, at, :], pair_of(0, chunks - 1, q)) + dot(
                skip_w[1, at, :], pair_of(2, chunks - 1, q)
            )
            skip_out[at, pl.ds(q * 2 * LANES, 2 * LANES)] = value.astype(BF)
        return carry

    lax.fori_loop(0, count, skip_step, 0)

    def second_one(k):
        wait_halo(3, k)
        at = pl.ds(pl.multiple_of(k * rows, rows), rows)
        for q in range(pairs):
            ybuf[at, pl.ds(q * 2 * LANES, 2 * LANES)] = mixed(1, 2, k, q)

    each(second_one)
    backward = ones_where((i0 % HALF) * channels + i0 // HALF == i1)
    for h in range(steps // HALF):
        value = dot(backward, ybuf[pl.ds(h * half_rows, half_rows), :]).astype(BF)
        next_out[:, pl.ds(h * HALF, HALF), :] = value.reshape(channels, HALF, width)

    for e in range(2 * LAYERS):

        def drain(k, e=e):
            for copy in halo(e, k):
                copy.wait_send()

        each(drain)


def on_device(
    series,
    caches,
    dilation,
    conv_weight,
    conv_bias,
    mix_weight,
    mix_bias,
    skip_weight,
    block_cols,
    block_count,
    edge_tiles,
):
    channels, steps, width = series.shape
    blocks, nonzero = block_cols.shape
    ring = lax.axis_size("sensor")
    reach = (nonzero - 1) // 2
    skips = skip_weight.shape[1]
    rows = CHUNK * channels
    chunks = steps // CHUNK
    caches = caches.transpose(0, 2, 1, 3).reshape(LAYERS, DMAX * channels, width)
    vmem, smem = pl.BlockSpec(memory_space=pltpu.VMEM), pl.BlockSpec(memory_space=pltpu.SMEM)
    following, skip = pl.pallas_call(
        functools.partial(kernel, blocks * ring, ring),
        out_shape=(
            jax.ShapeDtypeStruct((channels, steps, width), BF),
            jax.ShapeDtypeStruct((skips * SKT, width), BF),
        ),
        in_specs=[vmem, vmem, smem, vmem, vmem, vmem, vmem, vmem, smem, smem, vmem],
        out_specs=(vmem, vmem),
        scratch_shapes=[
            pltpu.VMEM((2 * LAYERS, blocks + 2 * reach, steps * channels, LANES), BF),
            pltpu.VMEM((LAYERS, (steps + DMAX) * channels, width), BF),
            pltpu.VMEM((steps * channels, width), BF),
            pltpu.VMEM((blocks // 2, (nonzero + 1) * LANES, 2 * LANES), BF),
            pltpu.VMEM((LAYERS, 2 * GROUP * channels, (GROUP + DMAX) * channels), BF),
            pltpu.VMEM((LAYERS, 2 * GROUP * channels, 1), F32),
            pltpu.VMEM((LAYERS, 3, rows, rows), BF),
            pltpu.VMEM((LAYERS, rows, 1), F32),
            pltpu.VMEM((LAYERS, skips * SKT, SKT * channels), BF),
            pltpu.SemaphoreType.DMA((2 * LAYERS, chunks, 2)),
            pltpu.SemaphoreType.DMA((2 * LAYERS, chunks, 2)),
        ],
        compiler_params=pltpu.CompilerParams(
            collective_id=0, has_side_effects=True, vmem_limit_bytes=48 * 2**20
        ),
    )(
        series,
        caches,
        dilation,
        conv_weight,
        conv_bias,
        mix_weight,
        mix_bias,
        skip_weight,
        block_cols,
        block_count,
        edge_tiles,
    )
    return following, skip.reshape(skips, SKT, width)


def solution(mesh):
    in_specs = (
        P(None, None, ("groups", "sensor")),
        P(None, None, None, ("groups", "sensor")),
        P(),
        P(),
        P(),
        P(),
        P(),
        P(),
        P(("groups", "sensor"), None),
        P(("groups", "sensor")),
        P(("groups", "sensor"), None, None, None),
    )
    out_specs = (P(None, None, ("groups", "sensor")), P(None, None, ("groups", "sensor")))
    return jax.shard_map(
        on_device, mesh=mesh, in_specs=in_specs, out_specs=out_specs, check_vma=False
    )
```

profile of v0, /device:TPU:1, one launch (start us, length us, event | category | flops | bytes accessed | tf_op | source)
XLA Modules:
  0.0 65.0 jit_solution(13513106283489196934)
XLA Ops:
  0.6 0.9 %copy.13 = bf16[2,2,32,512]{3,2,1,0:T(8,128)(2,1)S(1)} copy(bf16[2,2,32,512]{3,1,2,0:T(2,128)(2,1)} %bitcast.5) | data formatting | bytes 262144 | tf_op jit(solution)/shard_map/transpose | solution.py:332
  1.6 0.9 %copy.14.skip_weight = bf16[2,256,32]{2,1,0:T(8,128)(2,1)S(1)} copy(bf16[2,256,32]{1,2,0:T(8,128)(2,1)} %param.18) | data formatting | bytes 65536 | tf_op args[7]
  2.4 0.0 copy-start
  2.4 1.2 %copy-done = bf16[32,32,512]{2,1,0:T(8,128)(2,1)S(1)} copy-done((bf16[32,32,512]{2,1,0:T(8,128)(2,1)S(1)}, bf16[32,32,512]{2,1,0:T(8,128)(2,1)}, u32[]{:S(2)}) %copy-start) | copy-done | bytes 1048600
  3.7 0.0 copy-start.1
  3.7 1.1 %copy-done.1 = bf16[4,5,128,128]{3,2,1,0:T(8,128)(2,1)S(1)} copy-done((bf16[4,5,128,128]{3,2,1,0:T(8,128)(2,1)S(1)}, bf16[4,5,128,128]{3,2,1,0:T(8,128)(2,1)}, u32[]{:S(2)}) %copy-start.1) | copy-done | bytes 655384
  4.8 0.0 copy-start.2
  4.8 0.8 %copy-done.2 = bf16[2,4,32,32]{3,2,1,0:T(8,128)(2,1)S(1)} copy-done((bf16[2,4,32,32]{3,2,1,0:T(8,128)(2,1)S(1)}, bf16[2,4,32,32]{3,2,1,0:T(8,128)(2,1)}, u32[]{:S(2)}) %copy-start.2) | copy-done | bytes 16408
  5.6 0.0 copy-start.3
  5.6 0.8 %copy-done.3 = bf16[2,3,32,32]{3,2,1,0:T(8,128)(2,1)S(1)} copy-done((bf16[2,3,32,32]{3,2,1,0:T(8,128)(2,1)S(1)}, bf16[2,3,32,32]{3,2,1,0:T(8,128)(2,1)}, u32[]{:S(2)}) %copy-start.3) | copy-done | bytes 12312
  6.4 0.0 copy-start.4
  6.4 0.7 %copy-done.4 = f32[2,2,32]{2,1,0:T(2,128)S(1)} copy-done((f32[2,2,32]{2,1,0:T(2,128)S(1)}, f32[2,2,32]{2,1,0:T(2,128)}, u32[]{:S(2)}) %copy-start.4) | copy-done | bytes 536
  7.1 0.0 copy-start.5
  7.1 0.7 %copy-done.5 = s32[4,5]{1,0:T(4,128)S(1)} copy-done((s32[4,5]{1,0:T(4,128)S(1)}, s32[4,5]{1,0:T(4,128)}, u32[]{:S(2)}) %copy-start.5) | copy-done | bytes 104
  7.8 0.0 copy-start.6
  7.8 0.7 %copy-done.6 = f32[2,32]{1,0:T(2,128)S(1)} copy-done((f32[2,32]{1,0:T(2,128)S(1)}, f32[2,32]{1,0:T(2,128)}, u32[]{:S(2)}) %copy-start.6) | copy-done | bytes 280
  8.4 0.0 copy-start.7
  8.4 0.7 %copy-done.7 = s32[2]{0:T(128)S(1)} copy-done((s32[2]{0:T(128)S(1)}, s32[2]{0:T(128)}, u32[]{:S(2)}) %copy-start.7) | copy-done | bytes 32
  9.1 0.0 copy-start.8
  9.1 0.7 %copy-done.8 = s32[4]{0:T(128)S(1)} copy-done((s32[4]{0:T(128)S(1)}, s32[4]{0:T(128)}, u32[]{:S(2)}) %copy-start.8) | copy-done | bytes 40
  9.7 53.0 %shard_map.122 = (bf16[32,32,512]{2,1,0:T(8,128)(2,1)S(1)}, bf16[2048,512]{1,0:T(8,128)(2,1)S(1)}) custom-call(bf16[32,32,512]{2,1,0:T(8,128)(2,1)S(1)} %copy-done, bf16[2,64,512]{2,1,0:T(8,128)(2,1)S(1)} %bitcast.4, s32[2]{0:T(128)S(1)} %copy-done.7, bf16[2,4,32,32]{3,2,1,0:T(8,128)(2,1)S(1)} %copy-done.2, f32[2,2,32]{2,1,0:T(2,128)S(1)} %copy-done.4, ...), custom_call_target="tpu_custom_call" | custom-call | tf_op jit(solution)/shard_map/pallas_call | solution.py:334
  62.7 1.0 %copy.17 = bf16[32,32,512]{2,1,0:T(8,128)(2,1)} copy(bf16[32,32,512]{2,1,0:T(8,128)(2,1)S(1)} %get-tuple-element.8) | data formatting | bytes 2097152
  63.7 1.3 %copy.18 = bf16[256,8,512]{2,1,0:T(8,128)(2,1)} copy(bf16[256,8,512]{2,1,0:T(8,128)(2,1)S(1)} %bitcast.3) | data formatting | bytes 4194304
Async XLA Ops:
  2.4 1.2 %copy-start = (bf16[32,32,512]{2,1,0:T(8,128)(2,1)S(1)}, bf16[32,32,512]{2,1,0:T(8,128)(2,1)}, u32[]{:S(2)}) copy-start(bf16[32,32,512]{2,1,0:T(8,128)(2,1)} %series.1) | copy-start | bytes 3145732
  3.7 1.1 %copy-start.1 = (bf16[4,5,128,128]{3,2,1,0:T(8,128)(2,1)S(1)}, bf16[4,5,128,128]{3,2,1,0:T(8,128)(2,1)}, u32[]{:S(2)}) copy-start(bf16[4,5,128,128]{3,2,1,0:T(8,128)(2,1)} %edge_tiles.1) | copy-start | bytes 1966084
  4.8 0.8 %copy-start.2 = (bf16[2,4,32,32]{3,2,1,0:T(8,128)(2,1)S(1)}, bf16[2,4,32,32]{3,2,1,0:T(8,128)(2,1)}, u32[]{:S(2)}) copy-start(bf16[2,4,32,32]{3,2,1,0:T(8,128)(2,1)} %conv_weight.1) | copy-start | bytes 49156
  5.6 0.8 %copy-start.3 = (bf16[2,3,32,32]{3,2,1,0:T(8,128)(2,1)S(1)}, bf16[2,3,32,32]{3,2,1,0:T(8,128)(2,1)}, u32[]{:S(2)}) copy-start(bf16[2,3,32,32]{3,2,1,0:T(8,128)(2,1)} %mix_weight.1) | copy-start | bytes 36868
  6.4 0.7 %copy-start.4 = (f32[2,2,32]{2,1,0:T(2,128)S(1)}, f32[2,2,32]{2,1,0:T(2,128)}, u32[]{:S(2)}) copy-start(f32[2,2,32]{2,1,0:T(2,128)} %conv_bias.1) | copy-start | bytes 1540
  7.1 0.7 %copy-start.5 = (s32[4,5]{1,0:T(4,128)S(1)}, s32[4,5]{1,0:T(4,128)}, u32[]{:S(2)}) copy-start(s32[4,5]{1,0:T(4,128)} %block_cols.1) | copy-start | bytes 244
  7.8 0.7 %copy-start.6 = (f32[2,32]{1,0:T(2,128)S(1)}, f32[2,32]{1,0:T(2,128)}, u32[]{:S(2)}) copy-start(f32[2,32]{1,0:T(2,128)} %mix_bias.1) | copy-start | bytes 772
  8.4 0.7 %copy-start.7 = (s32[2]{0:T(128)S(1)}, s32[2]{0:T(128)}, u32[]{:S(2)}) copy-start(s32[2]{0:T(128)} %dilation.1) | copy-start | bytes 28
  9.1 0.7 %copy-start.8 = (s32[4]{0:T(128)S(1)}, s32[4]{0:T(128)}, u32[]{:S(2)}) copy-start(s32[4]{0:T(128)} %block_count.1) | copy-start | bytes 52
where the time goes:
time: 65.5 us; the launch traced here: 65 us
  Pallas kernels  53 us (81%)
  local copies, waits for them, and re-layouts  11.4 us (17%)
  between operations  0.66 us (1%)
    pallas_call x1, Pallas kernels, on_device(): pl.pallas_call(functools.partial(kernel, blocks * ring, ring), out_shape=...  53 us
    unnamed x21, local copies, waits for them, and re-layouts  10.5 us

commit v1 on v0

--- a/solution.py
+++ b/solution.py
@@ -46,17 +46,19 @@
 def kernel(
     total_blocks,
     ring,
-    series,
-    caches,
-    dilation,
-    conv_weight,
-    conv_bias,
-    mix_weight,
-    mix_bias,
-    skip_weight,
-    block_cols,
-    block_count,
-    edge_tiles,
+    series_in,
+    caches_in,
+    dilation_in,
+    conv_weight_in,
+    conv_bias_in,
+    mix_weight_in,
+    mix_bias_in,
+    skip_weight_in,
+    block_cols_in,
+    block_count_in,
+    edge_tiles_in,
+    next_hbm,
+    skip_hbm,
     next_out,
     skip_out,
     ext,
@@ -70,6 +72,19 @@
     skip_w,
     send_sem,
     recv_sem,
+    load_sem,
+    store_sem,
+    series,
+    caches,
+    dilation,
+    conv_weight,
+    conv_bias,
+    mix_weight,
+    mix_bias,
+    skip_weight,
+    block_cols,
+    block_count,
+    edge_tiles,
 ):
     channels, steps, width = series.shape
     blocks = width // LANES
@@ -80,6 +95,31 @@
     own = reach
     me = lax.axis_index("sensor")
     left, right = lax.rem(me + ring - 1, ring), lax.rem(me + 1, ring)
+
+    halves = steps // HALF
+    loads = [
+        pltpu.make_async_copy(
+            series_in.at[:, pl.ds(h * HALF, HALF), :],
+            series.at[:, pl.ds(h * HALF, HALF), :],
+            load_sem.at[h],
+        )
+        for h in range(halves)
+    ]
+    for source, target in (
+        (conv_weight_in, conv_weight),
+        (conv_bias_in, conv_bias),
+        (dilation_in, dilation),
+        (caches_in, caches),
+        (edge_tiles_in, edge_tiles),
+        (block_cols_in, block_cols),
+        (block_count_in, block_count),
+        (mix_weight_in, mix_weight),
+        (mix_bias_in, mix_bias),
+        (skip_weight_in, skip_weight),
+    ):
+        loads.append(pltpu.make_async_copy(source, target, load_sem.at[len(loads)]))
+    for load in loads:
+        load.start()
 
     barrier = pltpu.get_barrier_semaphore()
     for other in (left, right):
@@ -126,10 +166,10 @@
         mix_b[l] = column(mix_bias[pl.ds(l, 1), :], rows)
 
     def build_skip(l):
-        o, c = skip_weight.shape[1:]
+        c, o = skip_weight.shape[1:]
         piece = 512
         wide = ones_where(iota((c, SKT * c), 1) % c == iota((c, SKT * c), 0))
-        repeated = dot(skip_weight[l], wide).astype(BF)
+        repeated = dot(skip_weight[l].astype(F32).T.astype(BF), wide).astype(BF)
 
         def step(i, carry):
             tall = ones_where(
@@ -223,26 +263,36 @@
 
         lax.fori_loop(0, chunks, step, 0)
 
+    def each_half(h, step):
+        per = HALF // CHUNK
+        lax.fori_loop(h * per, (h + 1) * per, step, 0)
+
     half_rows = HALF * channels
     square = (half_rows, half_rows)
+    i0, i1 = iota(square, 0), iota(square, 1)
+    forward = ones_where((i0 % channels) * HALF + i0 // channels == i1)
+    for load in loads[halves : halves + 4]:
+        load.wait()
+    build_conv(0)
     for l in range(LAYERS):
         xbuf[l, pl.ds(0, DMAX * channels), :] = caches[l]
-    build_conv(0)
-    i0, i1 = iota(square, 0), iota(square, 1)
-    forward = ones_where((i0 % channels) * HALF + i0 // channels == i1)
-    for h in range(steps // HALF):
+
+    def hidden_zero(k, carry):
+        gated(0, 0, k)
+        start_halo(0, k)
+        return carry
+
+    for h in range(halves):
+        loads[h].wait()
         piece = series[:, pl.ds(h * HALF, HALF), :].reshape(half_rows, width)
         xbuf[0, pl.ds(DMAX * channels + h * half_rows, half_rows), :] = dot(
             forward, piece
         ).astype(BF)
-
-    pl.semaphore_wait(barrier, 2)
-
-    def hidden_zero(k):
-        gated(0, 0, k)
-        start_halo(0, k)
-
-    each(hidden_zero)
+        if h == 0:
+            pl.semaphore_wait(barrier, 2)
+        each_half(h, hidden_zero)
+    for load in loads[halves + 4 :]:
+        load.wait()
     build_plan()
     build_conv(1)
     build_mix(0)
@@ -287,18 +337,30 @@
         return carry
 
     lax.fori_loop(0, count, skip_step, 0)
-
-    def second_one(k):
+    stores = [pltpu.make_async_copy(skip_out, skip_hbm, store_sem.at[halves])]
+    stores[0].start()
+
+    backward = ones_where((i0 % HALF) * channels + i0 // HALF == i1)
+
+    def second_one(k, carry):
         wait_halo(3, k)
         at = pl.ds(pl.multiple_of(k * rows, rows), rows)
         for q in range(pairs):
             ybuf[at, pl.ds(q * 2 * LANES, 2 * LANES)] = mixed(1, 2, k, q)
-
-    each(second_one)
-    backward = ones_where((i0 % HALF) * channels + i0 // HALF == i1)
-    for h in range(steps // HALF):
+        return carry
+
+    for h in range(halves):
+        each_half(h, second_one)
         value = dot(backward, ybuf[pl.ds(h * half_rows, half_rows), :]).astype(BF)
         next_out[:, pl.ds(h * HALF, HALF), :] = value.reshape(channels, HALF, width)
+        stores.append(
+            pltpu.make_async_copy(
+                next_out.at[:, pl.ds(h * HALF, HALF), :],
+                next_hbm.at[:, pl.ds(h * HALF, HALF), :],
+                store_sem.at[h],
+            )
+        )
+        stores[-1].start()
 
     for e in range(2 * LAYERS):
 
@@ -307,6 +369,8 @@
                 copy.wait_send()
 
         each(drain)
+    for store in stores:
+        store.wait()
 
 
 def on_device(
@@ -330,32 +394,9 @@
     rows = CHUNK * channels
     chunks = steps // CHUNK
     caches = caches.transpose(0, 2, 1, 3).reshape(LAYERS, DMAX * channels, width)
-    vmem, smem = pl.BlockSpec(memory_space=pltpu.VMEM), pl.BlockSpec(memory_space=pltpu.SMEM)
-    following, skip = pl.pallas_call(
-        functools.partial(kernel, blocks * ring, ring),
-        out_shape=(
-            jax.ShapeDtypeStruct((channels, steps, width), BF),
-            jax.ShapeDtypeStruct((skips * SKT, width), BF),
-        ),
-        in_specs=[vmem, vmem, smem, vmem, vmem, vmem, vmem, vmem, smem, smem, vmem],
-        out_specs=(vmem, vmem),
-        scratch_shapes=[
-            pltpu.VMEM((2 * LAYERS, blocks + 2 * reach, steps * channels, LANES), BF),
-            pltpu.VMEM((LAYERS, (steps + DMAX) * channels, width), BF),
-            pltpu.VMEM((steps * channels, width), BF),
-            pltpu.VMEM((blocks // 2, (nonzero + 1) * LANES, 2 * LANES), BF),
-            pltpu.VMEM((LAYERS, 2 * GROUP * channels, (GROUP + DMAX) * channels), BF),
-            pltpu.VMEM((LAYERS, 2 * GROUP * channels, 1), F32),
-            pltpu.VMEM((LAYERS, 3, rows, rows), BF),
-            pltpu.VMEM((LAYERS, rows, 1), F32),
-            pltpu.VMEM((LAYERS, skips * SKT, SKT * channels), BF),
-            pltpu.SemaphoreType.DMA((2 * LAYERS, chunks, 2)),
-            pltpu.SemaphoreType.DMA((2 * LAYERS, chunks, 2)),
-        ],
-        compiler_params=pltpu.CompilerParams(
-            collective_id=0, has_side_effects=True, vmem_limit_bytes=48 * 2**20
-        ),
-    )(
+    skip_weight = skip_weight.transpose(0, 2, 1)
+    hbm = pl.BlockSpec(memory_space=pltpu.HBM)
+    operands = (
         series,
         caches,
         dilation,
@@ -368,6 +409,42 @@
         block_count,
         edge_tiles,
     )
+    small = (2, 8, 9)
+    places = [
+        (pltpu.SMEM if i in small else pltpu.VMEM)(x.shape, x.dtype)
+        for i, x in enumerate(operands)
+    ]
+    loads = len(operands) - 1 + steps // HALF
+    following, skip = pl.pallas_call(
+        functools.partial(kernel, blocks * ring, ring),
+        out_shape=(
+            jax.ShapeDtypeStruct((channels, steps, width), BF),
+            jax.ShapeDtypeStruct((skips * SKT, width), BF),
+        ),
+        in_specs=[hbm] * len(operands),
+        out_specs=(hbm, hbm),
+        scratch_shapes=[
+            pltpu.VMEM((channels, steps, width), BF),
+            pltpu.VMEM((skips * SKT, width), BF),
+            pltpu.VMEM((2 * LAYERS, blocks + 2 * reach, steps * channels, LANES), BF),
+            pltpu.VMEM((LAYERS, (steps + DMAX) * channels, width), BF),
+            pltpu.VMEM((steps * channels, width), BF),
+            pltpu.VMEM((blocks // 2, (nonzero + 1) * LANES, 2 * LANES), BF),
+            pltpu.VMEM((LAYERS, 2 * GROUP * channels, (GROUP + DMAX) * channels), BF),
+            pltpu.VMEM((LAYERS, 2 * GROUP * channels, 1), F32),
+            pltpu.VMEM((LAYERS, 3, rows, rows), BF),
+            pltpu.VMEM((LAYERS, rows, 1), F32),
+            pltpu.VMEM((LAYERS, skips * SKT, SKT * channels), BF),
+            pltpu.SemaphoreType.DMA((2 * LAYERS, chunks, 2)),
+            pltpu.SemaphoreType.DMA((2 * LAYERS, chunks, 2)),
+            pltpu.SemaphoreType.DMA((loads,)),
+            pltpu.SemaphoreType.DMA((steps // HALF + 1,)),
+            *places,
+        ],
+        compiler_params=pltpu.CompilerParams(
+            collective_id=0, has_side_effects=True, vmem_limit_bytes=60 * 2**20
+        ),
+    )(*operands)
     return following, skip.reshape(skips, SKT, width)
 
 

time: 65.5 us -> 60.2 us (0.919)
  local copies, waits for them, and re-layouts: 11.4 us -> 5.35 us
  Pallas kernels: 53 us -> 54.1 us
    unnamed x21 -> x4, local copies, waits for them, and re-layouts: 10.5 us -> 3.78 us
    pallas_call x1, Pallas kernels: 53 us -> 54.1 us  [on_device(): pl.pallas_call(functools.partial(kernel, blocks * ring, ring), out_shape=...]
where the time goes in v1:
time: 60.2 us; the launch traced here: 60.1 us
  Pallas kernels  54.1 us (90%)
  local copies, waits for them, and re-layouts  5.35 us (9%)
  between operations  0.65 us (1%)
    pallas_call x1, Pallas kernels, on_device(): pl.pallas_call(functools.partial(kernel, blocks * ring, ring), out_shape=...  54.1 us
    unnamed x4, local copies, waits for them, and re-layouts  3.78 us
    transpose x1, local copies, waits for them, and re-layouts, on_device(): caches.transpose(0, 2, 1, 3).reshape(LAYERS, DMAX * channels, width)  1.57 us

profile of v1, /device:TPU:1, one launch (start us, length us, event | category | flops | bytes accessed | tf_op | source)
XLA Modules:
  0.0 60.1 jit_solution(72942705943685954)
XLA Ops:
  0.6 1.6 %copy.13 = bf16[2,2,32,512]{3,2,1,0:T(8,128)(2,1)} copy(bf16[2,2,32,512]{3,1,2,0:T(2,128)(2,1)} %bitcast.6) | data formatting | bytes 262144 | tf_op jit(solution)/shard_map/transpose | solution.py:396
  2.2 54.1 %shard_map.122 = (bf16[32,32,512]{2,1,0:T(8,128)(2,1)}, bf16[2048,512]{1,0:T(8,128)(2,1)}) custom-call(bf16[32,32,512]{2,1,0:T(8,128)(2,1)} %series_in.1, bf16[2,64,512]{2,1,0:T(8,128)(2,1)} %bitcast.5, s32[2]{0:T(128)} %dilation_in.1, bf16[2,4,32,32]{3,2,1,0:T(8,128)(2,1)} %conv_weight_in.1, f32[2,2,32]{2,1,0:T(2,128)} %conv_bias_in.1, ...), custom_call_target="tpu_custom_call" | custom-call | tf_op jit(solution)/shard_map/pallas_call | solution.py:418
  56.3 0.0 copy-start
  56.3 2.5 %copy.16 = bf16[32,32,512]{2,1,0:T(8,128)(2,1)} copy(bf16[32,32,512]{2,1,0:T(8,128)(2,1)} %get-tuple-element.8) | data formatting | bytes 2097152
  58.8 0.0 copy-done
  58.8 1.3 %copy.17 = bf16[256,8,512]{2,1,0:T(8,128)(2,1)} copy(bf16[256,8,512]{2,1,0:T(8,128)(2,1)S(1)} %bitcast.4) | data formatting | bytes 4194304
Async XLA Ops:
  56.3 2.5 %copy-start = (bf16[2048,512]{1,0:T(8,128)(2,1)S(1)}, bf16[2048,512]{1,0:T(8,128)(2,1)}, u32[]{:S(2)}) copy-start(bf16[2048,512]{1,0:T(8,128)(2,1)} %get-tuple-element.5) | copy-start | bytes 6291460

commit v2 on v1

--- a/solution.py
+++ b/solution.py
@@ -59,7 +59,6 @@
     edge_tiles_in,
     next_hbm,
     skip_hbm,
-    next_out,
     skip_out,
     ext,
     xbuf,
@@ -275,7 +274,9 @@
         load.wait()
     build_conv(0)
     for l in range(LAYERS):
-        xbuf[l, pl.ds(0, DMAX * channels), :] = caches[l]
+        before = caches[l].astype(F32)
+        for t in range(DMAX):
+            xbuf[l, pl.ds(t * channels, channels), :] = before[:, t, :].astype(BF)
 
     def hidden_zero(k, carry):
         gated(0, 0, k)
@@ -337,30 +338,21 @@
         return carry
 
     lax.fori_loop(0, count, skip_step, 0)
-    stores = [pltpu.make_async_copy(skip_out, skip_hbm, store_sem.at[halves])]
-    stores[0].start()
-
-    backward = ones_where((i0 % HALF) * channels + i0 // HALF == i1)
-
-    def second_one(k, carry):
+    skip_store = pltpu.make_async_copy(skip_out, skip_hbm, store_sem.at[chunks])
+    skip_store.start()
+
+    def store(k):
+        at = pl.ds(pl.multiple_of(k * rows, rows), rows)
+        return pltpu.make_async_copy(ybuf.at[at, :], next_hbm.at[at, :], store_sem.at[k])
+
+    def second_one(k):
         wait_halo(3, k)
         at = pl.ds(pl.multiple_of(k * rows, rows), rows)
         for q in range(pairs):
             ybuf[at, pl.ds(q * 2 * LANES, 2 * LANES)] = mixed(1, 2, k, q)
-        return carry
-
-    for h in range(halves):
-        each_half(h, second_one)
-        value = dot(backward, ybuf[pl.ds(h * half_rows, half_rows), :]).astype(BF)
-        next_out[:, pl.ds(h * HALF, HALF), :] = value.reshape(channels, HALF, width)
-        stores.append(
-            pltpu.make_async_copy(
-                next_out.at[:, pl.ds(h * HALF, HALF), :],
-                next_hbm.at[:, pl.ds(h * HALF, HALF), :],
-                store_sem.at[h],
-            )
-        )
-        stores[-1].start()
+        store(k).start()
+
+    each(second_one)
 
     for e in range(2 * LAYERS):
 
@@ -369,8 +361,8 @@
                 copy.wait_send()
 
         each(drain)
-    for store in stores:
-        store.wait()
+    each(lambda k: store(k).wait())
+    skip_store.wait()
 
 
 def on_device(
@@ -393,7 +385,6 @@
     skips = skip_weight.shape[1]
     rows = CHUNK * channels
     chunks = steps // CHUNK
-    caches = caches.transpose(0, 2, 1, 3).reshape(LAYERS, DMAX * channels, width)
     skip_weight = skip_weight.transpose(0, 2, 1)
     hbm = pl.BlockSpec(memory_space=pltpu.HBM)
     operands = (
@@ -418,13 +409,12 @@
     following, skip = pl.pallas_call(
         functools.partial(kernel, blocks * ring, ring),
         out_shape=(
-            jax.ShapeDtypeStruct((channels, steps, width), BF),
+            jax.ShapeDtypeStruct((steps * channels, width), BF),
             jax.ShapeDtypeStruct((skips * SKT, width), BF),
         ),
         in_specs=[hbm] * len(operands),
         out_specs=(hbm, hbm),
         scratch_shapes=[
-            pltpu.VMEM((channels, steps, width), BF),
             pltpu.VMEM((skips * SKT, width), BF),
             pltpu.VMEM((2 * LAYERS, blocks + 2 * reach, steps * channels, LANES), BF),
             pltpu.VMEM((LAYERS, (steps + DMAX) * channels, width), BF),
@@ -438,13 +428,14 @@
             pltpu.SemaphoreType.DMA((2 * LAYERS, chunks, 2)),
             pltpu.SemaphoreType.DMA((2 * LAYERS, chunks, 2)),
             pltpu.SemaphoreType.DMA((loads,)),
-            pltpu.SemaphoreType.DMA((steps // HALF + 1,)),
+            pltpu.SemaphoreType.DMA((chunks + 1,)),
             *places,
         ],
         compiler_params=pltpu.CompilerParams(
             collective_id=0, has_side_effects=True, vmem_limit_bytes=60 * 2**20
         ),
     )(*operands)
+    following = following.reshape(steps, channels, width).transpose(1, 0, 2)
     return following, skip.reshape(skips, SKT, width)
 
 

time: 60.2 us -> 59.1 us (0.982)
  local copies, waits for them, and re-layouts: 5.35 us -> 4.24 us
    reshape x0 -> x1, local copies, waits for them, and re-layouts: none -> 2.92 us  [on_device(): following = following.reshape(steps, channels, width).transpose(1, 0, 2)]
    unnamed x4 -> x3, local copies, waits for them, and re-layouts: 3.78 us -> 1.32 us
    transpose x1 -> x0, local copies, waits for them, and re-layouts: 1.57 us -> none  [on_device(): caches.transpose(0, 2, 1, 3).reshape(LAYERS, DMAX * channels, width)]
where the time goes in v2:
time: 59.1 us; the launch traced here: 58.9 us
  Pallas kernels  54 us (91%)
  local copies, waits for them, and re-layouts  4.24 us (7%)
  between operations  0.65 us (1%)
    pallas_call x1, Pallas kernels, on_device(): pl.pallas_call(functools.partial(kernel, blocks * ring, ring), out_shape=...  54 us
    reshape x1, local copies, waits for them, and re-layouts, on_device(): following = following.reshape(steps, channels, width).transpose(1, 0, 2)  2.92 us
    unnamed x3, local copies, waits for them, and re-layouts  1.32 us

profile of v2, /device:TPU:1, one launch (start us, length us, event | category | flops | bytes accessed | tf_op | source)
XLA Modules:
  0.0 58.9 jit_solution(11804257244536993261)
XLA Ops:
  0.6 54.0 %shard_map.122 = (bf16[1024,512]{1,0:T(8,128)(2,1)}, bf16[2048,512]{1,0:T(8,128)(2,1)}) custom-call(bf16[32,32,512]{2,1,0:T(8,128)(2,1)} %series_in.1, bf16[2,32,2,512]{3,2,1,0:T(2,128)(2,1)} %caches_in.1, s32[2]{0:T(128)} %dilation_in.1, bf16[2,4,32,32]{3,2,1,0:T(8,128)(2,1)} %conv_weight_in.1, f32[2,2,32]{2,1,0:T(2,128)} %conv_bias_in.1, ...), custom_call_target="tpu_custom_call" | custom-call | tf_op jit(solution)/shard_map/pallas_call | solution.py:409
  54.6 0.0 copy-start
  54.7 2.9 %copy.15 = bf16[32,32,512]{2,0,1:T(8,128)(2,1)} copy(bf16[32,32,512]{2,1,0:T(8,128)(2,1)} %bitcast.8) | data formatting | bytes 2097152 | tf_op jit(solution)/shard_map/reshape | solution.py:438
  57.6 0.0 copy-done
  57.6 1.3 %copy.17 = bf16[256,8,512]{2,1,0:T(8,128)(2,1)} copy(bf16[256,8,512]{2,1,0:T(8,128)(2,1)S(1)} %bitcast.6) | data formatting | bytes 4194304
Async XLA Ops:
  54.6 2.9 %copy-start = (bf16[2048,512]{1,0:T(8,128)(2,1)S(1)}, bf16[2048,512]{1,0:T(8,128)(2,1)}, u32[]{:S(2)}) copy-start(bf16[2048,512]{1,0:T(8,128)(2,1)} %get-tuple-element.5) | copy-start | bytes 6291460

commit v3 on v2

--- a/solution.py
+++ b/solution.py
@@ -363,6 +363,44 @@
         each(drain)
     each(lambda k: store(k).wait())
     skip_store.wait()
+
+
+def finish(y_in, skip_in, next_hbm, skip_hbm, y, out, skip, load_sem, store_sem):
+    channels, _, width = out.shape
+    rows = HALF * channels
+    halves = y.shape[0] // rows
+    part = skip.shape[0] // halves
+    y_at = [pl.ds(h * rows, rows) for h in range(halves)]
+    skip_at = [pl.ds(h * part, part) for h in range(halves)]
+    loads = [
+        pltpu.make_async_copy(y_in.at[at, :], y.at[at, :], load_sem.at[h])
+        for h, at in enumerate(y_at)
+    ] + [
+        pltpu.make_async_copy(skip_in.at[at, :], skip.at[at, :], load_sem.at[halves + h])
+        for h, at in enumerate(skip_at)
+    ]
+    for load in loads:
+        load.start()
+    i0, i1 = iota((rows, rows), 0), iota((rows, rows), 1)
+    backward = ones_where((i0 % HALF) * channels + i0 // HALF == i1)
+    stores = []
+    for h in range(halves):
+        loads[h].wait()
+        value = dot(backward, y[y_at[h], :]).astype(BF)
+        times = pl.ds(h * HALF, HALF)
+        out[:, times, :] = value.reshape(channels, HALF, width)
+        stores.append(
+            pltpu.make_async_copy(out.at[:, times, :], next_hbm.at[:, times, :], store_sem.at[h])
+        )
+        stores[-1].start()
+    for h, at in enumerate(skip_at):
+        loads[halves + h].wait()
+        stores.append(
+            pltpu.make_async_copy(skip.at[at, :], skip_hbm.at[at, :], store_sem.at[halves + h])
+        )
+        stores[-1].start()
+    for store in stores:
+        store.wait()
 
 
 def on_device(
@@ -435,7 +473,24 @@
             collective_id=0, has_side_effects=True, vmem_limit_bytes=60 * 2**20
         ),
     )(*operands)
-    following = following.reshape(steps, channels, width).transpose(1, 0, 2)
+    halves = steps // HALF
+    following, skip = pl.pallas_call(
+        finish,
+        out_shape=(
+            jax.ShapeDtypeStruct((channels, steps, width), BF),
+            jax.ShapeDtypeStruct(skip.shape, BF),
+        ),
+        in_specs=[hbm, hbm],
+        out_specs=(hbm, hbm),
+        scratch_shapes=[
+            pltpu.VMEM(following.shape, BF),
+            pltpu.VMEM((channels, steps, width), BF),
+            pltpu.VMEM(skip.shape, BF),
+            pltpu.SemaphoreType.DMA((2 * halves,)),
+            pltpu.SemaphoreType.DMA((2 * halves,)),
+        ],
+        compiler_params=pltpu.CompilerParams(vmem_limit_bytes=60 * 2**20),
+    )(following, skip)
     return following, skip.reshape(skips, SKT, width)
 
 

time: 59.1 us -> 58.3 us (0.986)
  local copies, waits for them, and re-layouts: 4.24 us -> 0 us
  Pallas kernels: 54 us -> 57.5 us
    pallas_call x0 -> x1, Pallas kernels: none -> 3.48 us  [on_device(): pl.pallas_call(finish, out_shape=(jax.ShapeDtypeStruct((channels, steps,...]
    reshape x1 -> x0, local copies, waits for them, and re-layouts: 2.92 us -> none  [on_device(): following = following.reshape(steps, channels, width).transpose(1, 0, 2)]
    unnamed x3 -> x0, local copies, waits for them, and re-layouts: 1.32 us -> none
where the time goes in v3:
time: 58.3 us; the launch traced here: 58.1 us
  Pallas kernels  57.5 us (99%)
  between operations  0.64 us (1%)
    pallas_call x1, Pallas kernels, on_device(): pl.pallas_call(functools.partial(kernel, blocks * ring, ring), out_shape=...  54 us
    pallas_call x1, Pallas kernels, on_device(): pl.pallas_call(finish, out_shape=(jax.ShapeDtypeStruct((channels, steps,...  3.48 us

profile of v3, /device:TPU:1, one launch (start us, length us, event | category | flops | bytes accessed | tf_op | source)
XLA Modules:
  0.0 58.1 jit_solution(15964192579690968609)
XLA Ops:
  0.6 54.0 %shard_map.122 = (bf16[1024,512]{1,0:T(8,128)(2,1)}, bf16[2048,512]{1,0:T(8,128)(2,1)}) custom-call(bf16[32,32,512]{2,1,0:T(8,128)(2,1)} %series_in.1, bf16[2,32,2,512]{3,2,1,0:T(2,128)(2,1)} %caches_in.1, s32[2]{0:T(128)} %dilation_in.1, bf16[2,4,32,32]{3,2,1,0:T(8,128)(2,1)} %conv_weight_in.1, f32[2,2,32]{2,1,0:T(2,128)} %conv_bias_in.1, ...), custom_call_target="tpu_custom_call" | custom-call | tf_op jit(solution)/shard_map/pallas_call | solution.py:447
  54.6 3.5 %shard_map.123 = (bf16[32,32,512]{2,1,0:T(8,128)(2,1)}, bf16[2048,512]{1,0:T(8,128)(2,1)}) custom-call(bf16[1024,512]{1,0:T(8,128)(2,1)} %get-tuple-element.6.y_in, bf16[2048,512]{1,0:T(8,128)(2,1)} %get-tuple-element.7.skip_in), custom_call_target="tpu_custom_call" | custom-call | tf_op jit(solution)/shard_map/pallas_call | solution.py:477

commit v4 on v3

--- a/solution.py
+++ b/solution.py
@@ -11,7 +11,7 @@
 DMAX = 2
 SKT = 8
 LANES = 128
-CHUNK = 8
+CHUNK = 4
 GROUP = 4
 HALF = 16
 BF = jnp.bfloat16
@@ -235,6 +235,12 @@
             [ext[e, own + 2 * q, at, :], ext[e, own + 2 * q + 1, at, :]], axis=1
         )
 
+    def tail_of(e, q):
+        at = pl.ds((steps - SKT) * channels, SKT * channels)
+        return jnp.concatenate(
+            [ext[e, own + 2 * q, at, :], ext[e, own + 2 * q + 1, at, :]], axis=1
+        )
+
     def mixed(l, e, k, q):
         cols = pl.ds(q * 2 * LANES, 2 * LANES)
         second = diffused(e + 1, k, q)
@@ -331,9 +337,7 @@
     def skip_step(i, carry):
         at = pl.ds(pl.multiple_of(i * piece, piece), piece)
         for q in range(pairs):
-            value = dot(skip_w[0, at, :], pair_of(0, chunks - 1, q)) + dot(
-                skip_w[1, at, :], pair_of(2, chunks - 1, q)
-            )
+            value = dot(skip_w[0, at, :], tail_of(0, q)) + dot(skip_w[1, at, :], tail_of(2, q))
             skip_out[at, pl.ds(q * 2 * LANES, 2 * LANES)] = value.astype(BF)
         return carry
 

time: 58.3 us -> 60.5 us (1.038)
  Pallas kernels: 57.5 us -> 59.7 us
    pallas_call x1, Pallas kernels: 54 us -> 56.2 us  [on_device(): pl.pallas_call(functools.partial(kernel, blocks * ring, ring), out_shape=...]
where the time goes in v4:
time: 60.5 us; the launch traced here: 60.3 us
  Pallas kernels  59.7 us (99%)
  between operations  0.64 us (1%)
    pallas_call x1, Pallas kernels, on_device(): pl.pallas_call(functools.partial(kernel, blocks * ring, ring), out_shape=...  56.2 us
    pallas_call x1, Pallas kernels, on_device(): pl.pallas_call(finish, out_shape=(jax.ShapeDtypeStruct((channels, steps,...  3.48 us

profile of v4, /device:TPU:1, one launch (start us, length us, event | category | flops | bytes accessed | tf_op | source)
XLA Modules:
  0.0 60.3 jit_solution(8242031572937044258)
XLA Ops:
  0.6 56.2 %shard_map.122 = (bf16[1024,512]{1,0:T(8,128)(2,1)}, bf16[2048,512]{1,0:T(8,128)(2,1)}) custom-call(bf16[32,32,512]{2,1,0:T(8,128)(2,1)} %series_in.1, bf16[2,32,2,512]{3,2,1,0:T(2,128)(2,1)} %caches_in.1, s32[2]{0:T(128)} %dilation_in.1, bf16[2,4,32,32]{3,2,1,0:T(8,128)(2,1)} %conv_weight_in.1, f32[2,2,32]{2,1,0:T(2,128)} %conv_bias_in.1, ...), custom_call_target="tpu_custom_call" | custom-call | tf_op jit(solution)/shard_map/pallas_call | solution.py:451
  56.8 3.5 %shard_map.123 = (bf16[32,32,512]{2,1,0:T(8,128)(2,1)}, bf16[2048,512]{1,0:T(8,128)(2,1)}) custom-call(bf16[1024,512]{1,0:T(8,128)(2,1)} %get-tuple-element.6.y_in, bf16[2048,512]{1,0:T(8,128)(2,1)} %get-tuple-element.7.skip_in), custom_call_target="tpu_custom_call" | custom-call | tf_op jit(solution)/shard_map/pallas_call | solution.py:481
